TPU v7x, 32 devices: a whole 2x2x4 slice. The times are simulated.
32 devices in a mesh: sx: 4 (over x, core), sy: 4 (over z), ch: 2 (over y).
Axes of the slice: x: 2, y: 2, z: 4, core: 2. Of those that a mesh axis runs over, the one named last changes fastest.
Arguments:
- volume: bfloat16 [512, 32, 512], P('ch', 'sx', 'sy'), may hold values from -6 to 6
- weight: bfloat16 [3, 3, 3, 512, 512], P(None, None, None, 'ch'), may hold values from -0.0546875 to 0.0546875
- bias: float32 [512], P('ch'), may hold values from -3 to 3
Outputs:
- convolved: bfloat16 [512, 32, 512], P('ch', 'sx', 'sy')
All inputs are finite; a program needn't handle non-finite values.
Results may differ from a plain program's by a relative error of at most 0.001.
Values may be sent and summed in bfloat16 or wider, within the bound.
No kernel may reach another device: no remote copies, remote signals or barrier semaphores. Data moves between devices by JAX's collectives and lax.ppermute only.
A program may use at most 192 MiB of HBM per device.

v0:
```python
import functools

import jax
import jax.numpy as jnp
from jax import lax
from jax.experimental import pallas as pl
from jax.experimental.pallas import tpu as pltpu
from jax.sharding import PartitionSpec as P

CZ = 16
LANES = 128
VMEM = pl.BlockSpec(memory_space=pltpu.VMEM)
HBM = pl.BlockSpec(memory_space=pltpu.HBM)
ANY = pl.BlockSpec(memory_space=pl.ANY)
bf16, f32 = jnp.bfloat16, jnp.float32


def call(kernel, outs, args, scratch=(), left={}, limit=24, flops=0, out=VMEM):
    return pl.pallas_call(
        kernel,
        out_shape=[jax.ShapeDtypeStruct(s, d) for s, d in outs],
        in_specs=[left.get(i, VMEM) for i in range(len(args))],
        out_specs=[out] * len(outs),
        scratch_shapes=list(scratch),
        compiler_params=pltpu.CompilerParams(vmem_limit_bytes=limit * 2**20),
        cost_estimate=pl.CostEstimate(flops=flops, bytes_accessed=0, transcendentals=0),
    )(*args)


def swap_near(count):
    return [i ^ 1 for i in range(count)]


def swap_far(count):
    return [None, *[i + 1 if i % 2 else i - 1 for i in range(1, count - 1)], None]


def exchange(block, axis, other, far):
    count, width = lax.axis_size(axis), lax.axis_size(other)
    partner = swap_far(count) if far else swap_near(count)
    aside = swap_near(width)
    moves = []
    for i in range(count):
        for j in range(width):
            to = (i, aside[j]) if partner[i] is None else (partner[i], j)
            if axis == "sx":
                moves.append((i * width + j, to[0] * width + to[1]))
            else:
                moves.append((j * count + i, to[1] * count + to[0]))
    return lax.ppermute(block, ("sx", "sy"), moves)


def pass_on(block, step):
    count_x, count_y, count = (lax.axis_size(a) for a in ("sx", "sy", "ch"))
    moves = []
    for x in range(count_x):
        for y in range(count_y):
            for c in range(count):
                to = (y ^ 1, c) if x in (0, count_x - 1) else (y, (c + step) % count)
                moves.append(((x * count_y + y) * count + c, (x * count_y + to[0]) * count + to[1]))
    return lax.ppermute(block, ("sx", "sy", "ch"), moves)


def odd(axis):
    return lax.rem(lax.axis_index(axis), 2) == 1


def at_end(axis):
    at = lax.axis_index(axis)
    return jnp.logical_or(at == 0, at == lax.axis_size(axis) - 1)


def ready_kernel(out_ref):
    out_ref[...] = jnp.zeros_like(out_ref)


def to_rows(edges, v_ref, *refs):
    rows_ref, near_ref, *far_ref = refs[len(refs) - 1 - edges :]
    rows = jnp.swapaxes(v_ref[...], 0, 1)
    rows_ref[...] = rows
    is_odd = odd("sx")
    near_ref[...] = jnp.where(is_odd, rows[0], rows[-1])
    if far_ref:
        far_ref[0][...] = jnp.where(is_odd, rows[-1], rows[0])


def around(axis, near, far):
    is_odd = odd(axis)
    far = jnp.where(at_end(axis), jnp.zeros_like(far), far)
    return jnp.where(is_odd, near, far), jnp.where(is_odd, far, near)


def extended(rows_ref, near_ref, far_ref):
    before, after = around("sx", near_ref[...], far_ref[...])
    return [before, *[rows_ref[x] for x in range(rows_ref.shape[0])], after]


def pack(rows, start):
    cut = [r[:, start : start + CZ] for r in rows]
    part = rows[0].shape[0] // 4
    outer = jnp.concatenate([cut[0], cut[-1]], axis=1)
    folded = jnp.concatenate([outer[g * part : (g + 1) * part] for g in range(4)], axis=1)
    return jnp.concatenate([jnp.concatenate(cut[1:-1], axis=1), folded], axis=0)


def to_strips(rows_ref, near_ref, far_ref, _, near_strip_ref, far_strip_ref):
    rows = extended(rows_ref, near_ref, far_ref)
    low = pack(rows, 0)
    high = pack(rows, LANES - CZ)
    is_odd = odd("sy")
    near_strip_ref[...] = jnp.where(is_odd, low, high)
    far_strip_ref[...] = jnp.where(is_odd, high, low)


def inner_rows(cells_x):
    return list(range(1, cells_x - 1))


def shift_along_y(row, xs, x):
    lanes = row.shape[1]
    lane = lax.broadcasted_iota(jnp.int32, row.shape, 1)
    wide = row.astype(f32)
    xs[0, x] = jnp.where(lane < CZ, 0.0, pltpu.roll(wide, CZ, axis=1)).astype(bf16)
    xs[1, x] = jnp.where(lane >= lanes - CZ, 0.0, pltpu.roll(wide, lanes - CZ, axis=1)).astype(bf16)


def taps_of(weight_ref, a, b, step, channels, low=0, high=None):
    high = high or weight_ref.shape[3]
    outputs = pl.ds(low, high - low)
    if channels % LANES:
        taps = weight_ref[a, b, :, outputs, step * channels : (step + 1) * channels]
    else:
        count = lax.axis_size("ch")
        at = lax.rem(lax.axis_index("ch") + count - step, count)
        start = pl.multiple_of(at * channels, channels)
        taps = weight_ref[a, b, :, outputs, pl.ds(start, channels)]
    return taps.reshape(3 * (high - low), channels)


def tile_sum(weight_ref, step, rows, xs, tile, along_y, total=None):
    for b in along_y:
        for a in range(3):
            window = [rows[x + a] if b == 1 else xs[b // 2, x + a] for x in tile]
            rhs = jnp.concatenate(window, axis=1)
            taps = taps_of(weight_ref, a, b, step, rhs.shape[0])
            product = jnp.dot(taps, rhs, preferred_element_type=f32)
            total = product if total is None else total + product
    return total


def split(total):
    return [total[:, j : j + LANES] for j in range(0, total.shape[1], LANES)]


def strip_windows(strips_ref, channels):
    lanes, part = LANES, channels // 4
    size = channels + part
    near, far = strips_ref[0:size].astype(f32), strips_ref[size : 2 * size].astype(f32)
    lane = lax.broadcasted_iota(jnp.int32, (channels, lanes), 1)
    ends = []
    for strip in around("sy", near, far):
        main, folded = strip[:channels], strip[channels:]
        first, last = (
            jnp.concatenate(
                [pltpu.roll(folded, (to - at - g * 2 * CZ) % lanes, axis=1) for g in range(4)],
                axis=0,
            )
            for to, at in ((0, 0), (lanes - CZ, CZ))
        )
        windows = [
            jnp.where(lane < CZ, first, pltpu.roll(main, CZ, axis=1)),
            main,
            jnp.where(lane >= lanes - CZ, last, pltpu.roll(main, lanes - CZ, axis=1)),
        ]
        ends.append([w.astype(bf16) for w in windows])
    return ends


def strip_sums(weight_ref, step, ends, low=0, high=None):
    sums = []
    for b, windows in zip((0, 2), ends):
        total = None
        for a in range(3):
            taps = taps_of(weight_ref, a, b, step, windows[a].shape[0], low, high)
            product = jnp.dot(taps, windows[a], preferred_element_type=f32)
            total = product if total is None else total + product
        sums.append(total)
    return sums


def combine(row):
    outputs = row.shape[0] // 3
    cell = lax.rem(lax.broadcasted_iota(jnp.int32, (outputs, LANES), 1), CZ)
    under, mid, over = (row[c * outputs : (c + 1) * outputs] for c in range(3))
    under = jnp.where(cell == 0, 0.0, pltpu.roll(under, 1, axis=1))
    over = jnp.where(cell == CZ - 1, 0.0, pltpu.roll(over, LANES - 1, axis=1))
    return (under + over) + mid


def first_kernel(rows_ref, weight_ref, sum_ref, xs):
    cells_x = rows_ref.shape[0]
    rows = [None, *[rows_ref[x] for x in range(cells_x)]]
    tile = inner_rows(cells_x)[: sum_ref.shape[0]]
    for x in range(tile[0], tile[-1] + 3):
        shift_along_y(rows[x], xs, x)
    total = tile_sum(weight_ref, 0, rows, xs, tile, (1, 0, 2))
    for j, part in enumerate(split(total)):
        sum_ref[j] = part


def second_kernel(rows_ref, near_ref, far_ref, weight_ref, sum_ref, xs):
    rows = extended(rows_ref, near_ref, far_ref)
    last = rows_ref.shape[0] - 1
    done = rows_ref.shape[0] - sum_ref.shape[0]
    left = [*inner_rows(last + 1)[done:], 0, last]
    for x in range(last + 3):
        if any(x - a in left for a in range(3)):
            shift_along_y(rows[x], xs, x)
    for j in range(0, len(left), 2):
        total = tile_sum(weight_ref, 0, rows, xs, left[j : j + 2], (1, 0, 2))
        for i, part in enumerate(split(total)):
            sum_ref[j + i] = part


def join_kernel(near_ref, far_ref, far_row_ref, _, strips_ref):
    size = near_ref.shape[0]
    strips_ref[0:size] = near_ref[...]
    strips_ref[size : 2 * size] = far_ref[...]
    strips_ref[2 * size :] = far_row_ref[...]


def ends_kernel(strips_ref, weight_ref, near_ref, ends_ref):
    windows = strip_windows(strips_ref, near_ref.shape[0])
    for j, part in enumerate(strip_sums(weight_ref, 0, windows)):
        ends_ref[j] = part


def inner_kernel(others, *refs):
    weight_ref, one_ref, two_ref, bias_ref, *refs = refs
    rows_refs, (sum_ref, xs) = refs[:others], refs[others:]
    cells_x = rows_refs[0].shape[0]
    order = inner_rows(cells_x)
    totals = [None] * (len(order) // 2)
    for i in range(others):
        rows = [None, *[rows_refs[i][x] for x in range(cells_x)]]
        for x in range(1, cells_x + 1):
            shift_along_y(rows[x], xs, x)
        for j in range(len(totals)):
            tile = order[2 * j : 2 * j + 2]
            totals[j] = tile_sum(weight_ref, i + 1, rows, xs, tile, (1, 0, 2), totals[j])
    kept = one_ref.shape[0]
    for j, part in enumerate(part for total in totals for part in split(total)):
        own = one_ref[j] if j < kept else two_ref[j - kept]
        sum_ref[j] = combine(own + part) + bias_ref[...]


def outer_kernel(others, *refs):
    weight_ref, two_ref, bias_ref, _, *refs = refs
    rows_refs, near_refs = refs[:others], refs[others : 2 * others]
    sum_ref, xs = refs[2 * others :]
    last = rows_refs[0].shape[0] - 1
    total = None
    for i in range(others):
        near = near_refs[i][...]
        before, after = around("sx", near, jnp.zeros_like(near))
        rows = [before, *[rows_refs[i][x] for x in range(last + 1)], after]
        for x in (0, 1, 2, last, last + 1, last + 2):
            shift_along_y(rows[x], xs, x)
        total = tile_sum(weight_ref, i + 1, rows, xs, (0, last), (1, 0, 2), total)
    done = two_ref.shape[0] - 2
    for j, part in enumerate(split(total)):
        sum_ref[j] = combine(two_ref[done + j] + part) + bias_ref[...]


def last_kernel(others, *refs):
    inner_ref, outer_ref, ends_ref, weight_ref, *passed_refs = refs[: 4 + others]
    out_ref, xs, stage, sems = refs[4 + others :]
    outputs, cells_x, lanes = stage.shape
    channels = xs.shape[2]
    is_odd = odd("sx")
    far_tap = jnp.where(is_odd, 2, 0)
    ends, fars = [], []
    for i, ref in enumerate(passed_refs):
        ends.append(strip_windows(ref, channels))
        far = ref[pl.ds(ref.shape[0] - channels, channels)]
        far = jnp.where(at_end("sx"), jnp.zeros_like(far), far)
        shift_along_y(far, xs, i)
        fars.append(far)
    pieces = 2 if outputs % 32 == 0 else 1
    size = outputs // pieces
    lane = lax.broadcasted_iota(jnp.int32, (size, lanes), 1)
    copies = []
    for p in range(pieces):
        low, high = p * size, (p + 1) * size
        sums = [
            jnp.concatenate(
                [ends_ref[j, c * outputs + low : c * outputs + high] for c in range(3)], axis=0
            )
            for j in range(2)
        ]
        edge = None
        for i in range(others):
            parts = strip_sums(weight_ref, i + 1, ends[i], low, high)
            sums = [s + part for s, part in zip(sums, parts)]
            for b in range(3):
                taps = taps_of(weight_ref, far_tap, b, i + 1, channels, low, high)
                window = fars[i] if b == 1 else xs[b // 2, i]
                product = jnp.dot(taps, window, preferred_element_type=f32)
                edge = product if edge is None else edge + product
        first_end, last_end = (combine(s) for s in sums)
        edge = combine(edge)
        rows = []
        for x in range(cells_x):
            first = pltpu.roll(first_end, (-x * CZ) % lanes, axis=1)
            final = pltpu.roll(last_end, (lanes - CZ - x * CZ) % lanes, axis=1)
            kept = outer_ref.at[x and 1] if x in (0, cells_x - 1) else inner_ref.at[x - 1]
            row = kept[low:high]
            if x == 0:
                row = row + jnp.where(is_odd, 0.0, edge)
            if x == cells_x - 1:
                row = row + jnp.where(is_odd, edge, 0.0)
            row = row + jnp.where(lane < CZ, first, jnp.where(lane >= lanes - CZ, final, 0.0))
            rows.append(row.astype(bf16))
        stage[low:high] = jnp.swapaxes(jnp.stack(rows), 0, 1)
        copies.append(
            pltpu.make_async_copy(stage.at[low:high], out_ref.at[low:high], sems.at[p])
        )
        copies[-1].start()
    for copy in copies:
        copy.wait()


def per_device(volume, weight, bias):
    channels, cells_x, lanes = volume.shape
    outputs = weight.shape[3]
    count = lax.axis_size("ch")
    others = count - 1
    strip = channels + channels // 4
    face, taps = (channels, lanes), (3 * outputs, lanes)
    half = cells_x // 2
    xs = pltpu.VMEM((2, cells_x + 2, *face), bf16)

    def along(step):
        return [(i, (i + step) % count) for i in range(count)]

    def rows_of(block, edges, *after):
        return call(
            functools.partial(to_rows, edges),
            [((cells_x, *face), bf16)] + [(face, bf16)] * edges,
            [block, *after],
            left={1: ANY},
            flops=(edges - 1) * 10**10,
        )

    other_raw = [lax.ppermute(volume, "ch", along(step)) for step in range(1, count)]
    spread = jnp.broadcast_to(bias[:, None], (outputs, lanes))
    if channels % LANES:
        at = lax.axis_index("ch")
        blocks = [lax.rem(at + count - step, count) * channels for step in range(count)]
        weight = jnp.concatenate(
            [lax.dynamic_slice_in_dim(weight, i, channels, axis=4) for i in blocks], axis=4
        )
    (ready,) = call(ready_kernel, [((8, lanes), f32)], [], flops=10**10)
    rows, near, far = rows_of(volume, 2, ready)
    near = exchange(near, "sx", "sy", False)
    far = exchange(far, "sx", "sy", True)
    (one,) = call(first_kernel, [((half, *taps), f32)], [rows, weight], [xs])
    low, high = call(to_strips, [((strip, lanes), bf16)] * 2, [rows, near, far, one], left={3: ANY})
    low = exchange(low, "sy", "sx", False)
    high = exchange(high, "sy", "sx", True)
    (two,) = call(
        second_kernel,
        [((cells_x - half, *taps), f32)],
        [rows, near, far, weight],
        [xs],
    )
    (strips,) = call(join_kernel, [((2 * strip + channels, lanes), bf16)], [low, high, far, two], left={3: ANY})
    other_strips = [lax.ppermute(strips, "ch", along(step)) for step in range(1, count)]
    (ends,) = call(ends_kernel, [((2, *taps), f32)], [strips, weight, near])
    other_rows, other_near = [], []
    for raw in other_raw:
        moved, edge = rows_of(raw, 1, ends)
        other_rows.append(moved)
        other_near.append(exchange(edge, "sx", "sy", False))
    (inner,) = call(
        functools.partial(inner_kernel, others),
        [((cells_x - 2, outputs, lanes), f32)],
        [weight, one, two, spread, *other_rows],
        [xs],
    )
    (outer,) = call(
        functools.partial(outer_kernel, others),
        [((2, outputs, lanes), f32)],
        [weight, two, spread, inner, *other_rows, *other_near],
        [xs],
        left={3: ANY},
    )
    return call(
        functools.partial(last_kernel, others),
        [((outputs, cells_x, lanes), bf16)],
        [inner, outer, ends, weight, *other_strips],
        [
            pltpu.VMEM((2, others, *face), bf16),
            pltpu.VMEM((outputs, cells_x, lanes), bf16),
            pltpu.SemaphoreType.DMA((2,)),
        ],
        out=HBM,
    )[0]


def solution(mesh):
    return jax.shard_map(
        per_device,
        mesh=mesh,
        in_specs=(P("ch", "sx", "sy"), P(None, None, None, "ch", None), P("ch")),
        out_specs=P("ch", "sx", "sy"),
        check_vma=False,
    )
```

profile of v0, /device:TPU:0, one launch (start us, length us, event | category | flops | bytes accessed | tf_op | source)
XLA Modules:
  0.0 22.7 jit_solution(5408277283862319347)
XLA Ops:
  0.0 0.0 copy-start
  0.0 3.0 %collective-permute-start.2 = (bf16[256,8,128]{2,1,0:T(8,128)(2,1)}, bf16[256,8,128]{2,1,0:T(8,128)(2,1)S(1)}, u32[]{:S(2)}, u32[]{:S(2)}) collective-permute-start(bf16[256,8,128]{2,1,0:T(8,128)(2,1)} %v_ref.1), channel_id=1, source_target_pairs={{0,1},{1,0},{2,3},{3,2},{4,5},{5,4},{6,7},{7,6},{8,9},{9,8},{10,11... | collective-permute-start | bytes 1572872 | tf_op jit(solution)/shard_map/ppermute | solution.py:355
  3.0 0.0 slice-start
  3.0 0.0 copy-done
  3.0 0.0 slice-start.1
  3.0 0.1 shard_map.38
  3.1 0.1 collective-permute-start
  3.2 1.6 %collective-permute-start.1 = (bf16[256,128]{1,0:T(8,128)(2,1)S(1)}, bf16[256,128]{1,0:T(8,128)(2,1)S(1)}, u32[]{:S(2)}, u32[]{:S(2)}) collective-permute-start(bf16[256,128]{1,0:T(8,128)(2,1)S(1)} %get-tuple-element.14), channel_id=1, source_target_pairs={{0,2},{2,0},{4,6},{6,4},{8,16},{10,18},{12,20},{14,22},{16,8},{18,... | collective-permute-start | bytes 196616 | tf_op jit(solution)/shard_map/ppermute | solution.py:50
  4.8 0.3 %slice-done = s8[4194304]{0:T(1024)(128)(4,1)S(1)} async-done(((s8[7077888]{0:T(1024)(128)(4,1)}), s8[4194304]{0:T(1024)(128)(4,1)S(1)}, s32[]{:S(2)}) %slice-start) | async-done | bytes 4194328
  5.2 0.9 %slice-done.1 = s8[2883584]{0:T(1024)(128)(4,1)S(1)} async-done(((s8[7077888]{0:T(1024)(128)(4,1)}), s8[2883584]{0:T(1024)(128)(4,1)S(1)}, s32[]{:S(2)}) %slice-start.1) | async-done | bytes 2883608
  6.1 2.0 %shard_map.39._.refs_1_ = f32[4,768,128]{2,1,0:T(8,128)S(1)} custom-call(bf16[8,256,128]{2,1,0:T(8,128)(2,1)S(1)} %get-tuple-element.12.rows_ref, bf16[3,3,3,256,512]{4,3,2,1,0:T(8,128)(2,1)S(1)} %bitcast.1), custom_call_target="tpu_custom_call" | custom-call | tf_op jit(solution)/shard_map/pallas_call | solution.py:19
  8.1 0.0 collective-permute-done.near_ref
  8.1 0.0 collective-permute-done.1.far_ref.far_row_ref
  8.1 0.5 %shard_map.41 = (bf16[320,128]{1,0:T(8,128)(2,1)S(1)}, bf16[320,128]{1,0:T(8,128)(2,1)S(1)}) custom-call(bf16[8,256,128]{2,1,0:T(8,128)(2,1)S(1)} %get-tuple-element.12.rows_ref, bf16[256,128]{1,0:T(8,128)(2,1)S(1)} %collective-permute-done.near_ref, bf16[256,128]{1,0:T(8,128)(2,1)S(1)} %collective-permute-done.1.far_ref.far_row_ref, ...), custom_call_target="tpu_custom_call" | custom-call | tf_op jit(solution)/shard_map/pallas_call | solution.py:19
  8.6 1.6 %collective-permute-start.3 = (bf16[320,128]{1,0:T(8,128)(2,1)S(1)}, bf16[320,128]{1,0:T(8,128)(2,1)S(1)}, u32[]{:S(2)}, u32[]{:S(2)}) collective-permute-start(bf16[320,128]{1,0:T(8,128)(2,1)S(1)} %get-tuple-element.15), channel_id=1, source_target_pairs={{0,2},{8,10},{16,18},{24,26},{2,0},{10,8},{18,16},{26,24},{4,6},{1... | collective-permute-start | bytes 245768 | tf_op jit(solution)/shard_map/ppermute | solution.py:50
  10.2 0.0 collective-permute-start.4
  10.2 2.1 %shard_map.40._.refs_2_.refs_1_ = f32[4,768,128]{2,1,0:T(8,128)S(1)} custom-call(bf16[8,256,128]{2,1,0:T(8,128)(2,1)S(1)} %get-tuple-element.12.rows_ref, bf16[256,128]{1,0:T(8,128)(2,1)S(1)} %collective-permute-done.near_ref, bf16[256,128]{1,0:T(8,128)(2,1)S(1)} %collective-permute-done.1.far_ref.far_row_ref, bf16[3,3,3,256,512]{4,3,2,1,0:T(8,128)(2,1)S(1)} %bitcast.1), custom_call_target="tpu_custom_call" | custom-call | tf_op jit(solution)/shard_map/pallas_call | solution.py:19
  12.3 0.8 %collective-permute-done.3.near_ref = bf16[320,128]{1,0:T(8,128)(2,1)S(1)} collective-permute-done((bf16[320,128]{1,0:T(8,128)(2,1)S(1)}, bf16[320,128]{1,0:T(8,128)(2,1)S(1)}, u32[]{:S(2)}, u32[]{:S(2)}) %collective-permute-start.3) | collective-permute-done | bytes 81952 | tf_op jit(solution)/shard_map/ppermute | solution.py:50
  13.1 0.0 collective-permute-done.4.far_ref
  13.1 0.0 copy-start.1
  13.1 0.5 %collective-permute-start.6 = (bf16[896,128]{1,0:T(8,128)(2,1)S(1)}, bf16[896,128]{1,0:T(8,128)(2,1)S(1)}, u32[]{:S(2)}, u32[]{:S(2)}) collective-permute-start(bf16[896,128]{1,0:T(8,128)(2,1)S(1)} %shard_map.42.strips_ref), channel_id=1, source_target_pairs={{0,1},{1,0},{2,3},{3,2},{4,5},{5,4},{6,7},{7,6},{8,9},{9,8},{10,11... | collective-permute-start | bytes 688136 | tf_op jit(solution)/shard_map/ppermute | solution.py:378
  13.7 0.8 %shard_map.43.refs_0_.refs_2_ = f32[2,768,128]{2,1,0:T(8,128)S(1)} custom-call(bf16[896,128]{1,0:T(8,128)(2,1)S(1)} %shard_map.42.strips_ref, bf16[3,3,3,256,512]{4,3,2,1,0:T(8,128)(2,1)S(1)} %bitcast.1, bf16[256,128]{1,0:T(8,128)(2,1)S(1)} %collective-permute-done.near_ref), custom_call_target="tpu_custom_call" | custom-call | tf_op jit(solution)/shard_map/pallas_call | solution.py:19
  14.5 0.7 %collective-permute-done.2.v_ref = bf16[256,8,128]{2,1,0:T(8,128)(2,1)S(1)} collective-permute-done((bf16[256,8,128]{2,1,0:T(8,128)(2,1)}, bf16[256,8,128]{2,1,0:T(8,128)(2,1)S(1)}, u32[]{:S(2)}, u32[]{:S(2)}) %collective-permute-start.2) | collective-permute-done | bytes 524320 | tf_op jit(solution)/shard_map/ppermute | solution.py:355
  15.2 0.1 shard_map.44
  15.3 0.1 collective-permute-start.5
  15.4 0.0 copy-done.1
  15.4 0.1 broadcast_in_dim.2.refs_3_.refs_2_
  15.5 3.1 %shard_map.45.refs_3_.refs_0_ = f32[6,256,128]{2,1,0:T(8,128)S(1)} custom-call(bf16[3,3,3,256,512]{4,3,2,1,0:T(8,128)(2,1)S(1)} %bitcast.1, f32[4,768,128]{2,1,0:T(8,128)S(1)} %shard_map.39._.refs_1_, f32[4,768,128]{2,1,0:T(8,128)S(1)} %shard_map.40._.refs_2_.refs_1_, f32[256,128]{1,0:T(8,128)S(1)} %broadcast_in_dim.2.refs_3_.refs_2_, ...), custom_call_target="tpu_custom_call" | custom-call | tf_op jit(solution)/shard_map/pallas_call | solution.py:19
  18.6 0.0 collective-permute-done.5.refs_5_
  18.6 1.3 %shard_map.46.refs_1_ = f32[2,256,128]{2,1,0:T(8,128)S(1)} custom-call(bf16[3,3,3,256,512]{4,3,2,1,0:T(8,128)(2,1)S(1)} %bitcast.1, f32[4,768,128]{2,1,0:T(8,128)S(1)} %shard_map.40._.refs_2_.refs_1_, f32[256,128]{1,0:T(8,128)S(1)} %broadcast_in_dim.2.refs_3_.refs_2_, f32[6,256,128]{2,1,0:T(8,128)S(1)} %shard_map.45.refs_3_.refs_0_, ...), custom_call_target="tpu_custom_call" | custom-call | tf_op jit(solution)/shard_map/pallas_call | solution.py:19
  19.9 0.5 %collective-permute-done.6.refs_4_ = bf16[896,128]{1,0:T(8,128)(2,1)S(1)} collective-permute-done((bf16[896,128]{1,0:T(8,128)(2,1)S(1)}, bf16[896,128]{1,0:T(8,128)(2,1)S(1)}, u32[]{:S(2)}, u32[]{:S(2)}) %collective-permute-start.6) | collective-permute-done | bytes 229408 | tf_op jit(solution)/shard_map/ppermute | solution.py:378
  20.4 2.2 %shard_map.47 = bf16[256,8,128]{2,1,0:T(8,128)(2,1)} custom-call(f32[6,256,128]{2,1,0:T(8,128)S(1)} %shard_map.45.refs_3_.refs_0_, f32[2,256,128]{2,1,0:T(8,128)S(1)} %shard_map.46.refs_1_, f32[2,768,128]{2,1,0:T(8,128)S(1)} %shard_map.43.refs_0_.refs_2_, bf16[3,3,3,256,512]{4,3,2,1,0:T(8,128)(2,1)S(1)} %bitcast.1, ...), custom_call_target="tpu_custom_call" | custom-call | tf_op jit(solution)/shard_map/pallas_call | solution.py:19
  (3 shorter events, 0.0 us)
Async XLA Ops:
  0.0 3.0 %copy-start = (bf16[256,8,128]{2,1,0:T(8,128)(2,1)S(1)}, bf16[256,8,128]{2,1,0:T(8,128)(2,1)}, u32[]{:S(2)}) copy-start(bf16[256,8,128]{2,1,0:T(8,128)(2,1)} %v_ref.1) | copy-start | bytes 1572868
  0.0 15.2 %collective-permute-start.2 = (bf16[256,8,128]{2,1,0:T(8,128)(2,1)}, bf16[256,8,128]{2,1,0:T(8,128)(2,1)S(1)}, u32[]{:S(2)}, u32[]{:S(2)}) collective-permute-start(bf16[256,8,128]{2,1,0:T(8,128)(2,1)} %v_ref.1), channel_id=1, source_target_pairs={{0,1},{1,0},{2,3},{3,2},{4,5},{5,4},{6,7},{7,6},{8,9},{9,8},{10,11... | collective-permute-start | bytes 1572872 | tf_op jit(solution)/shard_map/ppermute | solution.py:355
  3.0 2.2 %slice-start = ((s8[7077888]{0:T(1024)(128)(4,1)}), s8[4194304]{0:T(1024)(128)(4,1)S(1)}, s32[]{:S(2)}) async-start(s8[7077888]{0:T(1024)(128)(4,1)} %bitcast), calls=%async_computation | async-start | bytes 8388608
  3.0 3.1 %slice-start.1 = ((s8[7077888]{0:T(1024)(128)(4,1)}), s8[2883584]{0:T(1024)(128)(4,1)S(1)}, s32[]{:S(2)}) async-start(s8[7077888]{0:T(1024)(128)(4,1)} %bitcast), calls=%async_computation.1 | async-start | bytes 5767168
  3.1 5.0 %collective-permute-start = (bf16[256,128]{1,0:T(8,128)(2,1)S(1)}, bf16[256,128]{1,0:T(8,128)(2,1)S(1)}, u32[]{:S(2)}, u32[]{:S(2)}) collective-permute-start(bf16[256,128]{1,0:T(8,128)(2,1)S(1)} %get-tuple-element.13), channel_id=1, source_target_pairs={{0,8},{2,10},{4,12},{6,14},{8,0},{10,2},{12,4},{14,6},{16,24},{18,... | collective-permute-start | bytes 196616 | tf_op jit(solution)/shard_map/ppermute | solution.py:50
  3.2 4.9 %collective-permute-start.1 = (bf16[256,128]{1,0:T(8,128)(2,1)S(1)}, bf16[256,128]{1,0:T(8,128)(2,1)S(1)}, u32[]{:S(2)}, u32[]{:S(2)}) collective-permute-start(bf16[256,128]{1,0:T(8,128)(2,1)S(1)} %get-tuple-element.14), channel_id=1, source_target_pairs={{0,2},{2,0},{4,6},{6,4},{8,16},{10,18},{12,20},{14,22},{16,8},{18,... | collective-permute-start | bytes 196616 | tf_op jit(solution)/shard_map/ppermute | solution.py:50
  8.6 4.5 %collective-permute-start.3 = (bf16[320,128]{1,0:T(8,128)(2,1)S(1)}, bf16[320,128]{1,0:T(8,128)(2,1)S(1)}, u32[]{:S(2)}, u32[]{:S(2)}) collective-permute-start(bf16[320,128]{1,0:T(8,128)(2,1)S(1)} %get-tuple-element.15), channel_id=1, source_target_pairs={{0,2},{8,10},{16,18},{24,26},{2,0},{10,8},{18,16},{26,24},{4,6},{1... | collective-permute-start | bytes 245768 | tf_op jit(solution)/shard_map/ppermute | solution.py:50
  10.2 2.9 %collective-permute-start.4 = (bf16[320,128]{1,0:T(8,128)(2,1)S(1)}, bf16[320,128]{1,0:T(8,128)(2,1)S(1)}, u32[]{:S(2)}, u32[]{:S(2)}) collective-permute-start(bf16[320,128]{1,0:T(8,128)(2,1)S(1)} %get-tuple-element.16), channel_id=1, source_target_pairs={{0,8},{8,0},{16,24},{24,16},{2,4},{10,12},{18,20},{26,28},{4,2},{1... | collective-permute-start | bytes 245768 | tf_op jit(solution)/shard_map/ppermute | solution.py:50
  13.1 2.2 %copy-start.1 = (f32[256]{0:T(256)S(1)}, f32[256]{0:T(256)}, u32[]{:S(2)}) copy-start(f32[256]{0:T(256)} %param.5) | copy-start | bytes 3076
  13.1 7.3 %collective-permute-start.6 = (bf16[896,128]{1,0:T(8,128)(2,1)S(1)}, bf16[896,128]{1,0:T(8,128)(2,1)S(1)}, u32[]{:S(2)}, u32[]{:S(2)}) collective-permute-start(bf16[896,128]{1,0:T(8,128)(2,1)S(1)} %shard_map.42.strips_ref), channel_id=1, source_target_pairs={{0,1},{1,0},{2,3},{3,2},{4,5},{5,4},{6,7},{7,6},{8,9},{9,8},{10,11... | collective-permute-start | bytes 688136 | tf_op jit(solution)/shard_map/ppermute | solution.py:378
  15.3 3.3 %collective-permute-start.5 = (bf16[256,128]{1,0:T(8,128)(2,1)S(1)}, bf16[256,128]{1,0:T(8,128)(2,1)S(1)}, u32[]{:S(2)}, u32[]{:S(2)}) collective-permute-start(bf16[256,128]{1,0:T(8,128)(2,1)S(1)} %get-tuple-element.18), channel_id=1, source_target_pairs={{0,8},{2,10},{4,12},{6,14},{8,0},{10,2},{12,4},{14,6},{16,24},{18,... | collective-permute-start | bytes 196616 | tf_op jit(solution)/shard_map/ppermute | solution.py:50
where the time goes:
time: 22.8 us; the launch traced here: 22.7 us
  Pallas kernels  12.2 us (54%)
  starting transfers between devices  6.92 us (30%)
  waiting for transfers between devices  2.04 us (9%)
  local copies, waits for them, and re-layouts  1.34 us (6%)
    pallas_call x11, Pallas kernels, call(): pl.pallas_call(kernel, out_shape=[jax.ShapeDtypeStruct(s, d) for s, d in...  12.2 us
    ppermute x5, starting transfers between devices, exchange(): return lax.ppermute(block, ('sx', 'sy'), moves)  3.43 us
    ppermute x1, starting transfers between devices, per_device(): lax.ppermute(volume, 'ch', along(step))  2.97 us
    unnamed x8, local copies, waits for them, and re-layouts  1.26 us
    ppermute x5, waiting for transfers between devices, exchange(): return lax.ppermute(block, ('sx', 'sy'), moves)  0.81 us
    ppermute x1, waiting for transfers between devices, per_device(): lax.ppermute(volume, 'ch', along(step))  0.72 us
    ppermute x1, starting transfers between devices, per_device(): lax.ppermute(strips, 'ch', along(step))  0.53 us
    ppermute x1, waiting for transfers between devices, per_device(): lax.ppermute(strips, 'ch', along(step))  0.51 us
  transfers between devices with their start and end apart: 7, of which 3 were waited for; matrix products, arithmetic and copies ran while one was open for 0% of the time, Pallas kernels for 44%

commit v1 on v0

--- a/solution.py
+++ b/solution.py
@@ -10,17 +10,16 @@
 CZ = 16
 LANES = 128
 VMEM = pl.BlockSpec(memory_space=pltpu.VMEM)
-HBM = pl.BlockSpec(memory_space=pltpu.HBM)
 ANY = pl.BlockSpec(memory_space=pl.ANY)
 bf16, f32 = jnp.bfloat16, jnp.float32
 
 
-def call(kernel, outs, args, scratch=(), left={}, limit=24, flops=0, out=VMEM):
+def call(kernel, outs, args, scratch=(), left={}, limit=24, flops=0):
     return pl.pallas_call(
         kernel,
         out_shape=[jax.ShapeDtypeStruct(s, d) for s, d in outs],
         in_specs=[left.get(i, VMEM) for i in range(len(args))],
-        out_specs=[out] * len(outs),
+        out_specs=[VMEM] * len(outs),
         scratch_shapes=list(scratch),
         compiler_params=pltpu.CompilerParams(vmem_limit_bytes=limit * 2**20),
         cost_estimate=pl.CostEstimate(flops=flops, bytes_accessed=0, transcendentals=0),
@@ -274,8 +273,8 @@
 
 def last_kernel(others, *refs):
     inner_ref, outer_ref, ends_ref, weight_ref, *passed_refs = refs[: 4 + others]
-    out_ref, xs, stage, sems = refs[4 + others :]
-    outputs, cells_x, lanes = stage.shape
+    out_ref, xs = refs[4 + others :]
+    outputs, cells_x, lanes = out_ref.shape
     channels = xs.shape[2]
     is_odd = odd("sx")
     far_tap = jnp.where(is_odd, 2, 0)
@@ -289,7 +288,6 @@
     pieces = 2 if outputs % 32 == 0 else 1
     size = outputs // pieces
     lane = lax.broadcasted_iota(jnp.int32, (size, lanes), 1)
-    copies = []
     for p in range(pieces):
         low, high = p * size, (p + 1) * size
         sums = [
@@ -321,13 +319,7 @@
                 row = row + jnp.where(is_odd, edge, 0.0)
             row = row + jnp.where(lane < CZ, first, jnp.where(lane >= lanes - CZ, final, 0.0))
             rows.append(row.astype(bf16))
-        stage[low:high] = jnp.swapaxes(jnp.stack(rows), 0, 1)
-        copies.append(
-            pltpu.make_async_copy(stage.at[low:high], out_ref.at[low:high], sems.at[p])
-        )
-        copies[-1].start()
-    for copy in copies:
-        copy.wait()
+        out_ref[low:high] = jnp.swapaxes(jnp.stack(rows), 0, 1)
 
 
 def per_device(volume, weight, bias):
@@ -399,12 +391,7 @@
         functools.partial(last_kernel, others),
         [((outputs, cells_x, lanes), bf16)],
         [inner, outer, ends, weight, *other_strips],
-        [
-            pltpu.VMEM((2, others, *face), bf16),
-            pltpu.VMEM((outputs, cells_x, lanes), bf16),
-            pltpu.SemaphoreType.DMA((2,)),
-        ],
-        out=HBM,
+        [pltpu.VMEM((2, others, *face), bf16)],
     )[0]
 
 

time: 22.8 us -> 22.9 us (level)
  no operation moved by 1% of the time
where the time goes in v1:
time: 22.9 us; the launch traced here: 22.7 us
  Pallas kernels  12.3 us (54%)
  starting transfers between devices  6.92 us (30%)
  waiting for transfers between devices  2.04 us (9%)
  local copies, waits for them, and re-layouts  1.34 us (6%)
    pallas_call x11, Pallas kernels, call(): pl.pallas_call(kernel, out_shape=[jax.ShapeDtypeStruct(s, d) for s, d in...  12.3 us
    ppermute x5, starting transfers between devices, exchange(): return lax.ppermute(block, ('sx', 'sy'), moves)  3.43 us
    ppermute x1, starting transfers between devices, per_device(): lax.ppermute(volume, 'ch', along(step))  2.97 us
    unnamed x8, local copies, waits for them, and re-layouts  1.26 us
    ppermute x5, waiting for transfers between devices, exchange(): return lax.ppermute(block, ('sx', 'sy'), moves)  0.81 us
    ppermute x1, waiting for transfers between devices, per_device(): lax.ppermute(volume, 'ch', along(step))  0.72 us
    ppermute x1, starting transfers between devices, per_device(): lax.ppermute(strips, 'ch', along(step))  0.53 us
    ppermute x1, waiting for transfers between devices, per_device(): lax.ppermute(strips, 'ch', along(step))  0.51 us
  transfers between devices with their start and end apart: 7, of which 3 were waited for; matrix products, arithmetic and copies ran while one was open for 0% of the time, Pallas kernels for 44%

profile of v1, /device:TPU:0, one launch (start us, length us, event | category | flops | bytes accessed | tf_op | source)
XLA Modules:
  0.0 22.7 jit_solution(11606590946820831389)
XLA Ops:
  0.0 0.0 copy-start
  0.0 3.0 %collective-permute-start.2 = (bf16[256,8,128]{2,1,0:T(8,128)(2,1)}, bf16[256,8,128]{2,1,0:T(8,128)(2,1)S(1)}, u32[]{:S(2)}, u32[]{:S(2)}) collective-permute-start(bf16[256,8,128]{2,1,0:T(8,128)(2,1)} %v_ref.1), channel_id=1, source_target_pairs={{0,1},{1,0},{2,3},{3,2},{4,5},{5,4},{6,7},{7,6},{8,9},{9,8},{10,11... | collective-permute-start | bytes 1572872 | tf_op jit(solution)/shard_map/ppermute | solution.py:347
  3.0 0.0 slice-start
  3.0 0.0 copy-done
  3.0 0.0 slice-start.1
  3.0 0.1 shard_map.38
  3.1 0.1 collective-permute-start
  3.2 1.6 %collective-permute-start.1 = (bf16[256,128]{1,0:T(8,128)(2,1)S(1)}, bf16[256,128]{1,0:T(8,128)(2,1)S(1)}, u32[]{:S(2)}, u32[]{:S(2)}) collective-permute-start(bf16[256,128]{1,0:T(8,128)(2,1)S(1)} %get-tuple-element.14), channel_id=1, source_target_pairs={{0,2},{2,0},{4,6},{6,4},{8,16},{10,18},{12,20},{14,22},{16,8},{18,... | collective-permute-start | bytes 196616 | tf_op jit(solution)/shard_map/ppermute | solution.py:49
  4.8 0.3 %slice-done = s8[4194304]{0:T(1024)(128)(4,1)S(1)} async-done(((s8[7077888]{0:T(1024)(128)(4,1)}), s8[4194304]{0:T(1024)(128)(4,1)S(1)}, s32[]{:S(2)}) %slice-start) | async-done | bytes 4194328
  5.2 0.9 %slice-done.1 = s8[2883584]{0:T(1024)(128)(4,1)S(1)} async-done(((s8[7077888]{0:T(1024)(128)(4,1)}), s8[2883584]{0:T(1024)(128)(4,1)S(1)}, s32[]{:S(2)}) %slice-start.1) | async-done | bytes 2883608
  6.1 2.0 %shard_map.39._.refs_1_ = f32[4,768,128]{2,1,0:T(8,128)S(1)} custom-call(bf16[8,256,128]{2,1,0:T(8,128)(2,1)S(1)} %get-tuple-element.12.rows_ref, bf16[3,3,3,256,512]{4,3,2,1,0:T(8,128)(2,1)S(1)} %bitcast.1), custom_call_target="tpu_custom_call" | custom-call | tf_op jit(solution)/shard_map/pallas_call | solution.py:18
  8.1 0.0 collective-permute-done.near_ref
  8.1 0.0 collective-permute-done.1.far_ref.far_row_ref
  8.1 0.5 %shard_map.41 = (bf16[320,128]{1,0:T(8,128)(2,1)S(1)}, bf16[320,128]{1,0:T(8,128)(2,1)S(1)}) custom-call(bf16[8,256,128]{2,1,0:T(8,128)(2,1)S(1)} %get-tuple-element.12.rows_ref, bf16[256,128]{1,0:T(8,128)(2,1)S(1)} %collective-permute-done.near_ref, bf16[256,128]{1,0:T(8,128)(2,1)S(1)} %collective-permute-done.1.far_ref.far_row_ref, ...), custom_call_target="tpu_custom_call" | custom-call | tf_op jit(solution)/shard_map/pallas_call | solution.py:18
  8.6 1.6 %collective-permute-start.3 = (bf16[320,128]{1,0:T(8,128)(2,1)S(1)}, bf16[320,128]{1,0:T(8,128)(2,1)S(1)}, u32[]{:S(2)}, u32[]{:S(2)}) collective-permute-start(bf16[320,128]{1,0:T(8,128)(2,1)S(1)} %get-tuple-element.15), channel_id=1, source_target_pairs={{0,2},{8,10},{16,18},{24,26},{2,0},{10,8},{18,16},{26,24},{4,6},{1... | collective-permute-start | bytes 245768 | tf_op jit(solution)/shard_map/ppermute | solution.py:49
  10.2 0.0 collective-permute-start.4
  10.2 2.1 %shard_map.40._.refs_2_.refs_1_ = f32[4,768,128]{2,1,0:T(8,128)S(1)} custom-call(bf16[8,256,128]{2,1,0:T(8,128)(2,1)S(1)} %get-tuple-element.12.rows_ref, bf16[256,128]{1,0:T(8,128)(2,1)S(1)} %collective-permute-done.near_ref, bf16[256,128]{1,0:T(8,128)(2,1)S(1)} %collective-permute-done.1.far_ref.far_row_ref, bf16[3,3,3,256,512]{4,3,2,1,0:T(8,128)(2,1)S(1)} %bitcast.1), custom_call_target="tpu_custom_call" | custom-call | tf_op jit(solution)/shard_map/pallas_call | solution.py:18
  12.3 0.8 %collective-permute-done.3.near_ref = bf16[320,128]{1,0:T(8,128)(2,1)S(1)} collective-permute-done((bf16[320,128]{1,0:T(8,128)(2,1)S(1)}, bf16[320,128]{1,0:T(8,128)(2,1)S(1)}, u32[]{:S(2)}, u32[]{:S(2)}) %collective-permute-start.3) | collective-permute-done | bytes 81952 | tf_op jit(solution)/shard_map/ppermute | solution.py:49
  13.1 0.0 collective-permute-done.4.far_ref
  13.1 0.0 copy-start.1
  13.1 0.5 %collective-permute-start.6 = (bf16[896,128]{1,0:T(8,128)(2,1)S(1)}, bf16[896,128]{1,0:T(8,128)(2,1)S(1)}, u32[]{:S(2)}, u32[]{:S(2)}) collective-permute-start(bf16[896,128]{1,0:T(8,128)(2,1)S(1)} %shard_map.42.strips_ref), channel_id=1, source_target_pairs={{0,1},{1,0},{2,3},{3,2},{4,5},{5,4},{6,7},{7,6},{8,9},{9,8},{10,11... | collective-permute-start | bytes 688136 | tf_op jit(solution)/shard_map/ppermute | solution.py:370
  13.7 0.8 %shard_map.43.refs_0_.refs_2_ = f32[2,768,128]{2,1,0:T(8,128)S(1)} custom-call(bf16[896,128]{1,0:T(8,128)(2,1)S(1)} %shard_map.42.strips_ref, bf16[3,3,3,256,512]{4,3,2,1,0:T(8,128)(2,1)S(1)} %bitcast.1, bf16[256,128]{1,0:T(8,128)(2,1)S(1)} %collective-permute-done.near_ref), custom_call_target="tpu_custom_call" | custom-call | tf_op jit(solution)/shard_map/pallas_call | solution.py:18
  14.5 0.7 %collective-permute-done.2.v_ref = bf16[256,8,128]{2,1,0:T(8,128)(2,1)S(1)} collective-permute-done((bf16[256,8,128]{2,1,0:T(8,128)(2,1)}, bf16[256,8,128]{2,1,0:T(8,128)(2,1)S(1)}, u32[]{:S(2)}, u32[]{:S(2)}) %collective-permute-start.2) | collective-permute-done | bytes 524320 | tf_op jit(solution)/shard_map/ppermute | solution.py:347
  15.2 0.1 shard_map.44
  15.3 0.1 collective-permute-start.5
  15.4 0.0 copy-done.1
  15.4 0.1 broadcast_in_dim.2.refs_3_.refs_2_
  15.5 3.1 %shard_map.45.refs_3_.refs_0_ = f32[6,256,128]{2,1,0:T(8,128)S(1)} custom-call(bf16[3,3,3,256,512]{4,3,2,1,0:T(8,128)(2,1)S(1)} %bitcast.1, f32[4,768,128]{2,1,0:T(8,128)S(1)} %shard_map.39._.refs_1_, f32[4,768,128]{2,1,0:T(8,128)S(1)} %shard_map.40._.refs_2_.refs_1_, f32[256,128]{1,0:T(8,128)S(1)} %broadcast_in_dim.2.refs_3_.refs_2_, ...), custom_call_target="tpu_custom_call" | custom-call | tf_op jit(solution)/shard_map/pallas_call | solution.py:18
  18.6 0.0 collective-permute-done.5.refs_5_
  18.6 1.3 %shard_map.46.refs_1_ = f32[2,256,128]{2,1,0:T(8,128)S(1)} custom-call(bf16[3,3,3,256,512]{4,3,2,1,0:T(8,128)(2,1)S(1)} %bitcast.1, f32[4,768,128]{2,1,0:T(8,128)S(1)} %shard_map.40._.refs_2_.refs_1_, f32[256,128]{1,0:T(8,128)S(1)} %broadcast_in_dim.2.refs_3_.refs_2_, f32[6,256,128]{2,1,0:T(8,128)S(1)} %shard_map.45.refs_3_.refs_0_, ...), custom_call_target="tpu_custom_call" | custom-call | tf_op jit(solution)/shard_map/pallas_call | solution.py:18
  19.9 0.5 %collective-permute-done.6.refs_4_ = bf16[896,128]{1,0:T(8,128)(2,1)S(1)} collective-permute-done((bf16[896,128]{1,0:T(8,128)(2,1)S(1)}, bf16[896,128]{1,0:T(8,128)(2,1)S(1)}, u32[]{:S(2)}, u32[]{:S(2)}) %collective-permute-start.6) | collective-permute-done | bytes 229408 | tf_op jit(solution)/shard_map/ppermute | solution.py:370
  20.4 2.3 %shard_map.47 = bf16[256,8,128]{2,1,0:T(8,128)(2,1)} custom-call(f32[6,256,128]{2,1,0:T(8,128)S(1)} %shard_map.45.refs_3_.refs_0_, f32[2,256,128]{2,1,0:T(8,128)S(1)} %shard_map.46.refs_1_, f32[2,768,128]{2,1,0:T(8,128)S(1)} %shard_map.43.refs_0_.refs_2_, bf16[3,3,3,256,512]{4,3,2,1,0:T(8,128)(2,1)S(1)} %bitcast.1, ...), custom_call_target="tpu_custom_call" | custom-call | tf_op jit(solution)/shard_map/pallas_call | solution.py:18
  (3 shorter events, 0.0 us)
Async XLA Ops:
  0.0 3.0 %copy-start = (bf16[256,8,128]{2,1,0:T(8,128)(2,1)S(1)}, bf16[256,8,128]{2,1,0:T(8,128)(2,1)}, u32[]{:S(2)}) copy-start(bf16[256,8,128]{2,1,0:T(8,128)(2,1)} %v_ref.1) | copy-start | bytes 1572868
  0.0 15.2 %collective-permute-start.2 = (bf16[256,8,128]{2,1,0:T(8,128)(2,1)}, bf16[256,8,128]{2,1,0:T(8,128)(2,1)S(1)}, u32[]{:S(2)}, u32[]{:S(2)}) collective-permute-start(bf16[256,8,128]{2,1,0:T(8,128)(2,1)} %v_ref.1), channel_id=1, source_target_pairs={{0,1},{1,0},{2,3},{3,2},{4,5},{5,4},{6,7},{7,6},{8,9},{9,8},{10,11... | collective-permute-start | bytes 1572872 | tf_op jit(solution)/shard_map/ppermute | solution.py:347
  3.0 2.2 %slice-start = ((s8[7077888]{0:T(1024)(128)(4,1)}), s8[4194304]{0:T(1024)(128)(4,1)S(1)}, s32[]{:S(2)}) async-start(s8[7077888]{0:T(1024)(128)(4,1)} %bitcast), calls=%async_computation | async-start | bytes 8388608
  3.0 3.1 %slice-start.1 = ((s8[7077888]{0:T(1024)(128)(4,1)}), s8[2883584]{0:T(1024)(128)(4,1)S(1)}, s32[]{:S(2)}) async-start(s8[7077888]{0:T(1024)(128)(4,1)} %bitcast), calls=%async_computation.1 | async-start | bytes 5767168
  3.1 5.0 %collective-permute-start = (bf16[256,128]{1,0:T(8,128)(2,1)S(1)}, bf16[256,128]{1,0:T(8,128)(2,1)S(1)}, u32[]{:S(2)}, u32[]{:S(2)}) collective-permute-start(bf16[256,128]{1,0:T(8,128)(2,1)S(1)} %get-tuple-element.13), channel_id=1, source_target_pairs={{0,8},{2,10},{4,12},{6,14},{8,0},{10,2},{12,4},{14,6},{16,24},{18,... | collective-permute-start | bytes 196616 | tf_op jit(solution)/shard_map/ppermute | solution.py:49
  3.2 4.9 %collective-permute-start.1 = (bf16[256,128]{1,0:T(8,128)(2,1)S(1)}, bf16[256,128]{1,0:T(8,128)(2,1)S(1)}, u32[]{:S(2)}, u32[]{:S(2)}) collective-permute-start(bf16[256,128]{1,0:T(8,128)(2,1)S(1)} %get-tuple-element.14), channel_id=1, source_target_pairs={{0,2},{2,0},{4,6},{6,4},{8,16},{10,18},{12,20},{14,22},{16,8},{18,... | collective-permute-start | bytes 196616 | tf_op jit(solution)/shard_map/ppermute | solution.py:49
  8.6 4.5 %collective-permute-start.3 = (bf16[320,128]{1,0:T(8,128)(2,1)S(1)}, bf16[320,128]{1,0:T(8,128)(2,1)S(1)}, u32[]{:S(2)}, u32[]{:S(2)}) collective-permute-start(bf16[320,128]{1,0:T(8,128)(2,1)S(1)} %get-tuple-element.15), channel_id=1, source_target_pairs={{0,2},{8,10},{16,18},{24,26},{2,0},{10,8},{18,16},{26,24},{4,6},{1... | collective-permute-start | bytes 245768 | tf_op jit(solution)/shard_map/ppermute | solution.py:49
  10.2 2.9 %collective-permute-start.4 = (bf16[320,128]{1,0:T(8,128)(2,1)S(1)}, bf16[320,128]{1,0:T(8,128)(2,1)S(1)}, u32[]{:S(2)}, u32[]{:S(2)}) collective-permute-start(bf16[320,128]{1,0:T(8,128)(2,1)S(1)} %get-tuple-element.16), channel_id=1, source_target_pairs={{0,8},{8,0},{16,24},{24,16},{2,4},{10,12},{18,20},{26,28},{4,2},{1... | collective-permute-start | bytes 245768 | tf_op jit(solution)/shard_map/ppermute | solution.py:49
  13.1 2.2 %copy-start.1 = (f32[256]{0:T(256)S(1)}, f32[256]{0:T(256)}, u32[]{:S(2)}) copy-start(f32[256]{0:T(256)} %param.5) | copy-start | bytes 3076
  13.1 7.3 %collective-permute-start.6 = (bf16[896,128]{1,0:T(8,128)(2,1)S(1)}, bf16[896,128]{1,0:T(8,128)(2,1)S(1)}, u32[]{:S(2)}, u32[]{:S(2)}) collective-permute-start(bf16[896,128]{1,0:T(8,128)(2,1)S(1)} %shard_map.42.strips_ref), channel_id=1, source_target_pairs={{0,1},{1,0},{2,3},{3,2},{4,5},{5,4},{6,7},{7,6},{8,9},{9,8},{10,11... | collective-permute-start | bytes 688136 | tf_op jit(solution)/shard_map/ppermute | solution.py:370
  15.3 3.3 %collective-permute-start.5 = (bf16[256,128]{1,0:T(8,128)(2,1)S(1)}, bf16[256,128]{1,0:T(8,128)(2,1)S(1)}, u32[]{:S(2)}, u32[]{:S(2)}) collective-permute-start(bf16[256,128]{1,0:T(8,128)(2,1)S(1)} %get-tuple-element.18), channel_id=1, source_target_pairs={{0,8},{2,10},{4,12},{6,14},{8,0},{10,2},{12,4},{14,6},{16,24},{18,... | collective-permute-start | bytes 196616 | tf_op jit(solution)/shard_map/ppermute | solution.py:49

commit v2 on v1

--- a/solution.py
+++ b/solution.py
@@ -231,7 +231,7 @@
 def ends_kernel(strips_ref, weight_ref, near_ref, ends_ref):
     windows = strip_windows(strips_ref, near_ref.shape[0])
     for j, part in enumerate(strip_sums(weight_ref, 0, windows)):
-        ends_ref[j] = part
+        ends_ref[j] = combine(part)
 
 
 def inner_kernel(others, *refs):
@@ -290,22 +290,16 @@
     lane = lax.broadcasted_iota(jnp.int32, (size, lanes), 1)
     for p in range(pieces):
         low, high = p * size, (p + 1) * size
-        sums = [
-            jnp.concatenate(
-                [ends_ref[j, c * outputs + low : c * outputs + high] for c in range(3)], axis=0
-            )
-            for j in range(2)
-        ]
-        edge = None
+        sums = edge = None
         for i in range(others):
             parts = strip_sums(weight_ref, i + 1, ends[i], low, high)
-            sums = [s + part for s, part in zip(sums, parts)]
+            sums = [s + part for s, part in zip(sums, parts)] if sums else parts
             for b in range(3):
                 taps = taps_of(weight_ref, far_tap, b, i + 1, channels, low, high)
                 window = fars[i] if b == 1 else xs[b // 2, i]
                 product = jnp.dot(taps, window, preferred_element_type=f32)
                 edge = product if edge is None else edge + product
-        first_end, last_end = (combine(s) for s in sums)
+        first_end, last_end = (combine(s) + ends_ref[j, low:high] for j, s in enumerate(sums))
         edge = combine(edge)
         rows = []
         for x in range(cells_x):
@@ -368,7 +362,7 @@
     )
     (strips,) = call(join_kernel, [((2 * strip + channels, lanes), bf16)], [low, high, far, two], left={3: ANY})
     other_strips = [lax.ppermute(strips, "ch", along(step)) for step in range(1, count)]
-    (ends,) = call(ends_kernel, [((2, *taps), f32)], [strips, weight, near])
+    (ends,) = call(ends_kernel, [((2, outputs, lanes), f32)], [strips, weight, near])
     other_rows, other_near = [], []
     for raw in other_raw:
         moved, edge = rows_of(raw, 1, ends)

time: 22.9 us -> 22.8 us (level)
  no operation moved by 1% of the time
where the time goes in v2:
time: 22.8 us; the launch traced here: 22.7 us
  Pallas kernels  12.3 us (54%)
  starting transfers between devices  6.92 us (30%)
  waiting for transfers between devices  1.96 us (9%)
  local copies, waits for them, and re-layouts  1.34 us (6%)
    pallas_call x11, Pallas kernels, call(): pl.pallas_call(kernel, out_shape=[jax.ShapeDtypeStruct(s, d) for s, d in...  12.3 us
    ppermute x5, starting transfers between devices, exchange(): return lax.ppermute(block, ('sx', 'sy'), moves)  3.43 us
    ppermute x1, starting transfers between devices, per_device(): lax.ppermute(volume, 'ch', along(step))  2.97 us
    unnamed x8, local copies, waits for them, and re-layouts  1.26 us
    ppermute x5, waiting for transfers between devices, exchange(): return lax.ppermute(block, ('sx', 'sy'), moves)  0.81 us
    ppermute x1, waiting for transfers between devices, per_device(): lax.ppermute(volume, 'ch', along(step))  0.64 us
    ppermute x1, starting transfers between devices, per_device(): lax.ppermute(strips, 'ch', along(step))  0.53 us
    ppermute x1, waiting for transfers between devices, per_device(): lax.ppermute(strips, 'ch', along(step))  0.51 us
  transfers between devices with their start and end apart: 7, of which 3 were waited for; matrix products, arithmetic and copies ran while one was open for 0% of the time, Pallas kernels for 44%

profile of v2, /device:TPU:0, one launch (start us, length us, event | category | flops | bytes accessed | tf_op | source)
XLA Modules:
  0.0 22.7 jit_solution(5025923917848811638)
XLA Ops:
  0.0 0.0 copy-start
  0.0 3.0 %collective-permute-start.2 = (bf16[256,8,128]{2,1,0:T(8,128)(2,1)}, bf16[256,8,128]{2,1,0:T(8,128)(2,1)S(1)}, u32[]{:S(2)}, u32[]{:S(2)}) collective-permute-start(bf16[256,8,128]{2,1,0:T(8,128)(2,1)} %v_ref.1), channel_id=1, source_target_pairs={{0,1},{1,0},{2,3},{3,2},{4,5},{5,4},{6,7},{7,6},{8,9},{9,8},{10,11... | collective-permute-start | bytes 1572872 | tf_op jit(solution)/shard_map/ppermute | solution.py:341
  3.0 0.0 slice-start
  3.0 0.0 copy-done
  3.0 0.0 slice-start.1
  3.0 0.1 shard_map.38
  3.1 0.1 collective-permute-start
  3.2 1.6 %collective-permute-start.1 = (bf16[256,128]{1,0:T(8,128)(2,1)S(1)}, bf16[256,128]{1,0:T(8,128)(2,1)S(1)}, u32[]{:S(2)}, u32[]{:S(2)}) collective-permute-start(bf16[256,128]{1,0:T(8,128)(2,1)S(1)} %get-tuple-element.14), channel_id=1, source_target_pairs={{0,2},{2,0},{4,6},{6,4},{8,16},{10,18},{12,20},{14,22},{16,8},{18,... | collective-permute-start | bytes 196616 | tf_op jit(solution)/shard_map/ppermute | solution.py:49
  4.8 0.3 %slice-done = s8[4194304]{0:T(1024)(128)(4,1)S(1)} async-done(((s8[7077888]{0:T(1024)(128)(4,1)}), s8[4194304]{0:T(1024)(128)(4,1)S(1)}, s32[]{:S(2)}) %slice-start) | async-done | bytes 4194328
  5.2 0.9 %slice-done.1 = s8[2883584]{0:T(1024)(128)(4,1)S(1)} async-done(((s8[7077888]{0:T(1024)(128)(4,1)}), s8[2883584]{0:T(1024)(128)(4,1)S(1)}, s32[]{:S(2)}) %slice-start.1) | async-done | bytes 2883608
  6.1 2.0 %shard_map.39._.refs_1_ = f32[4,768,128]{2,1,0:T(8,128)S(1)} custom-call(bf16[8,256,128]{2,1,0:T(8,128)(2,1)S(1)} %get-tuple-element.12.rows_ref, bf16[3,3,3,256,512]{4,3,2,1,0:T(8,128)(2,1)S(1)} %bitcast.1), custom_call_target="tpu_custom_call" | custom-call | tf_op jit(solution)/shard_map/pallas_call | solution.py:18
  8.1 0.0 collective-permute-done.near_ref
  8.1 0.0 collective-permute-done.1.far_ref.far_row_ref
  8.1 0.5 %shard_map.41 = (bf16[320,128]{1,0:T(8,128)(2,1)S(1)}, bf16[320,128]{1,0:T(8,128)(2,1)S(1)}) custom-call(bf16[8,256,128]{2,1,0:T(8,128)(2,1)S(1)} %get-tuple-element.12.rows_ref, bf16[256,128]{1,0:T(8,128)(2,1)S(1)} %collective-permute-done.near_ref, bf16[256,128]{1,0:T(8,128)(2,1)S(1)} %collective-permute-done.1.far_ref.far_row_ref, ...), custom_call_target="tpu_custom_call" | custom-call | tf_op jit(solution)/shard_map/pallas_call | solution.py:18
  8.6 1.6 %collective-permute-start.3 = (bf16[320,128]{1,0:T(8,128)(2,1)S(1)}, bf16[320,128]{1,0:T(8,128)(2,1)S(1)}, u32[]{:S(2)}, u32[]{:S(2)}) collective-permute-start(bf16[320,128]{1,0:T(8,128)(2,1)S(1)} %get-tuple-element.15), channel_id=1, source_target_pairs={{0,2},{8,10},{16,18},{24,26},{2,0},{10,8},{18,16},{26,24},{4,6},{1... | collective-permute-start | bytes 245768 | tf_op jit(solution)/shard_map/ppermute | solution.py:49
  10.2 0.0 collective-permute-start.4
  10.2 2.1 %shard_map.40._.refs_2_.refs_1_ = f32[4,768,128]{2,1,0:T(8,128)S(1)} custom-call(bf16[8,256,128]{2,1,0:T(8,128)(2,1)S(1)} %get-tuple-element.12.rows_ref, bf16[256,128]{1,0:T(8,128)(2,1)S(1)} %collective-permute-done.near_ref, bf16[256,128]{1,0:T(8,128)(2,1)S(1)} %collective-permute-done.1.far_ref.far_row_ref, bf16[3,3,3,256,512]{4,3,2,1,0:T(8,128)(2,1)S(1)} %bitcast.1), custom_call_target="tpu_custom_call" | custom-call | tf_op jit(solution)/shard_map/pallas_call | solution.py:18
  12.3 0.8 %collective-permute-done.3.near_ref = bf16[320,128]{1,0:T(8,128)(2,1)S(1)} collective-permute-done((bf16[320,128]{1,0:T(8,128)(2,1)S(1)}, bf16[320,128]{1,0:T(8,128)(2,1)S(1)}, u32[]{:S(2)}, u32[]{:S(2)}) %collective-permute-start.3) | collective-permute-done | bytes 81952 | tf_op jit(solution)/shard_map/ppermute | solution.py:49
  13.1 0.0 collective-permute-done.4.far_ref
  13.1 0.0 copy-start.1
  13.1 0.5 %collective-permute-start.6 = (bf16[896,128]{1,0:T(8,128)(2,1)S(1)}, bf16[896,128]{1,0:T(8,128)(2,1)S(1)}, u32[]{:S(2)}, u32[]{:S(2)}) collective-permute-start(bf16[896,128]{1,0:T(8,128)(2,1)S(1)} %shard_map.42.strips_ref), channel_id=1, source_target_pairs={{0,1},{1,0},{2,3},{3,2},{4,5},{5,4},{6,7},{7,6},{8,9},{9,8},{10,11... | collective-permute-start | bytes 688136 | tf_op jit(solution)/shard_map/ppermute | solution.py:364
  13.7 0.9 %shard_map.43.refs_0_.refs_2_ = f32[2,256,128]{2,1,0:T(8,128)S(1)} custom-call(bf16[896,128]{1,0:T(8,128)(2,1)S(1)} %shard_map.42.strips_ref, bf16[3,3,3,256,512]{4,3,2,1,0:T(8,128)(2,1)S(1)} %bitcast.1, bf16[256,128]{1,0:T(8,128)(2,1)S(1)} %collective-permute-done.near_ref), custom_call_target="tpu_custom_call" | custom-call | tf_op jit(solution)/shard_map/pallas_call | solution.py:18
  14.5 0.6 %collective-permute-done.2.v_ref = bf16[256,8,128]{2,1,0:T(8,128)(2,1)S(1)} collective-permute-done((bf16[256,8,128]{2,1,0:T(8,128)(2,1)}, bf16[256,8,128]{2,1,0:T(8,128)(2,1)S(1)}, u32[]{:S(2)}, u32[]{:S(2)}) %collective-permute-start.2) | collective-permute-done | bytes 524320 | tf_op jit(solution)/shard_map/ppermute | solution.py:341
  15.2 0.1 shard_map.44
  15.3 0.1 collective-permute-start.5
  15.4 0.0 copy-done.1
  15.4 0.1 broadcast_in_dim.2.refs_3_.refs_2_
  15.5 3.1 %shard_map.45.refs_3_.refs_0_ = f32[6,256,128]{2,1,0:T(8,128)S(1)} custom-call(bf16[3,3,3,256,512]{4,3,2,1,0:T(8,128)(2,1)S(1)} %bitcast.1, f32[4,768,128]{2,1,0:T(8,128)S(1)} %shard_map.39._.refs_1_, f32[4,768,128]{2,1,0:T(8,128)S(1)} %shard_map.40._.refs_2_.refs_1_, f32[256,128]{1,0:T(8,128)S(1)} %broadcast_in_dim.2.refs_3_.refs_2_, ...), custom_call_target="tpu_custom_call" | custom-call | tf_op jit(solution)/shard_map/pallas_call | solution.py:18
  18.6 0.0 collective-permute-done.5.refs_5_
  18.6 1.3 %shard_map.46.refs_1_ = f32[2,256,128]{2,1,0:T(8,128)S(1)} custom-call(bf16[3,3,3,256,512]{4,3,2,1,0:T(8,128)(2,1)S(1)} %bitcast.1, f32[4,768,128]{2,1,0:T(8,128)S(1)} %shard_map.40._.refs_2_.refs_1_, f32[256,128]{1,0:T(8,128)S(1)} %broadcast_in_dim.2.refs_3_.refs_2_, f32[6,256,128]{2,1,0:T(8,128)S(1)} %shard_map.45.refs_3_.refs_0_, ...), custom_call_target="tpu_custom_call" | custom-call | tf_op jit(solution)/shard_map/pallas_call | solution.py:18
  19.9 0.5 %collective-permute-done.6.refs_4_ = bf16[896,128]{1,0:T(8,128)(2,1)S(1)} collective-permute-done((bf16[896,128]{1,0:T(8,128)(2,1)S(1)}, bf16[896,128]{1,0:T(8,128)(2,1)S(1)}, u32[]{:S(2)}, u32[]{:S(2)}) %collective-permute-start.6) | collective-permute-done | bytes 229408 | tf_op jit(solution)/shard_map/ppermute | solution.py:364
  20.4 2.2 %shard_map.47 = bf16[256,8,128]{2,1,0:T(8,128)(2,1)} custom-call(f32[6,256,128]{2,1,0:T(8,128)S(1)} %shard_map.45.refs_3_.refs_0_, f32[2,256,128]{2,1,0:T(8,128)S(1)} %shard_map.46.refs_1_, f32[2,256,128]{2,1,0:T(8,128)S(1)} %shard_map.43.refs_0_.refs_2_, bf16[3,3,3,256,512]{4,3,2,1,0:T(8,128)(2,1)S(1)} %bitcast.1, ...), custom_call_target="tpu_custom_call" | custom-call | tf_op jit(solution)/shard_map/pallas_call | solution.py:18
  (3 shorter events, 0.0 us)
Async XLA Ops:
  0.0 3.0 %copy-start = (bf16[256,8,128]{2,1,0:T(8,128)(2,1)S(1)}, bf16[256,8,128]{2,1,0:T(8,128)(2,1)}, u32[]{:S(2)}) copy-start(bf16[256,8,128]{2,1,0:T(8,128)(2,1)} %v_ref.1) | copy-start | bytes 1572868
  0.0 15.2 %collective-permute-start.2 = (bf16[256,8,128]{2,1,0:T(8,128)(2,1)}, bf16[256,8,128]{2,1,0:T(8,128)(2,1)S(1)}, u32[]{:S(2)}, u32[]{:S(2)}) collective-permute-start(bf16[256,8,128]{2,1,0:T(8,128)(2,1)} %v_ref.1), channel_id=1, source_target_pairs={{0,1},{1,0},{2,3},{3,2},{4,5},{5,4},{6,7},{7,6},{8,9},{9,8},{10,11... | collective-permute-start | bytes 1572872 | tf_op jit(solution)/shard_map/ppermute | solution.py:341
  3.0 2.2 %slice-start = ((s8[7077888]{0:T(1024)(128)(4,1)}), s8[4194304]{0:T(1024)(128)(4,1)S(1)}, s32[]{:S(2)}) async-start(s8[7077888]{0:T(1024)(128)(4,1)} %bitcast), calls=%async_computation | async-start | bytes 8388608
  3.0 3.1 %slice-start.1 = ((s8[7077888]{0:T(1024)(128)(4,1)}), s8[2883584]{0:T(1024)(128)(4,1)S(1)}, s32[]{:S(2)}) async-start(s8[7077888]{0:T(1024)(128)(4,1)} %bitcast), calls=%async_computation.1 | async-start | bytes 5767168
  3.1 5.0 %collective-permute-start = (bf16[256,128]{1,0:T(8,128)(2,1)S(1)}, bf16[256,128]{1,0:T(8,128)(2,1)S(1)}, u32[]{:S(2)}, u32[]{:S(2)}) collective-permute-start(bf16[256,128]{1,0:T(8,128)(2,1)S(1)} %get-tuple-element.13), channel_id=1, source_target_pairs={{0,8},{2,10},{4,12},{6,14},{8,0},{10,2},{12,4},{14,6},{16,24},{18,... | collective-permute-start | bytes 196616 | tf_op jit(solution)/shard_map/ppermute | solution.py:49
  3.2 4.9 %collective-permute-start.1 = (bf16[256,128]{1,0:T(8,128)(2,1)S(1)}, bf16[256,128]{1,0:T(8,128)(2,1)S(1)}, u32[]{:S(2)}, u32[]{:S(2)}) collective-permute-start(bf16[256,128]{1,0:T(8,128)(2,1)S(1)} %get-tuple-element.14), channel_id=1, source_target_pairs={{0,2},{2,0},{4,6},{6,4},{8,16},{10,18},{12,20},{14,22},{16,8},{18,... | collective-permute-start | bytes 196616 | tf_op jit(solution)/shard_map/ppermute | solution.py:49
  8.6 4.5 %collective-permute-start.3 = (bf16[320,128]{1,0:T(8,128)(2,1)S(1)}, bf16[320,128]{1,0:T(8,128)(2,1)S(1)}, u32[]{:S(2)}, u32[]{:S(2)}) collective-permute-start(bf16[320,128]{1,0:T(8,128)(2,1)S(1)} %get-tuple-element.15), channel_id=1, source_target_pairs={{0,2},{8,10},{16,18},{24,26},{2,0},{10,8},{18,16},{26,24},{4,6},{1... | collective-permute-start | bytes 245768 | tf_op jit(solution)/shard_map/ppermute | solution.py:49
  10.2 2.9 %collective-permute-start.4 = (bf16[320,128]{1,0:T(8,128)(2,1)S(1)}, bf16[320,128]{1,0:T(8,128)(2,1)S(1)}, u32[]{:S(2)}, u32[]{:S(2)}) collective-permute-start(bf16[320,128]{1,0:T(8,128)(2,1)S(1)} %get-tuple-element.16), channel_id=1, source_target_pairs={{0,8},{8,0},{16,24},{24,16},{2,4},{10,12},{18,20},{26,28},{4,2},{1... | collective-permute-start | bytes 245768 | tf_op jit(solution)/shard_map/ppermute | solution.py:49
  13.1 2.2 %copy-start.1 = (f32[256]{0:T(256)S(1)}, f32[256]{0:T(256)}, u32[]{:S(2)}) copy-start(f32[256]{0:T(256)} %param.5) | copy-start | bytes 3076
  13.1 7.3 %collective-permute-start.6 = (bf16[896,128]{1,0:T(8,128)(2,1)S(1)}, bf16[896,128]{1,0:T(8,128)(2,1)S(1)}, u32[]{:S(2)}, u32[]{:S(2)}) collective-permute-start(bf16[896,128]{1,0:T(8,128)(2,1)S(1)} %shard_map.42.strips_ref), channel_id=1, source_target_pairs={{0,1},{1,0},{2,3},{3,2},{4,5},{5,4},{6,7},{7,6},{8,9},{9,8},{10,11... | collective-permute-start | bytes 688136 | tf_op jit(solution)/shard_map/ppermute | solution.py:364
  15.3 3.3 %collective-permute-start.5 = (bf16[256,128]{1,0:T(8,128)(2,1)S(1)}, bf16[256,128]{1,0:T(8,128)(2,1)S(1)}, u32[]{:S(2)}, u32[]{:S(2)}) collective-permute-start(bf16[256,128]{1,0:T(8,128)(2,1)S(1)} %get-tuple-element.18), channel_id=1, source_target_pairs={{0,8},{2,10},{4,12},{6,14},{8,0},{10,2},{12,4},{14,6},{16,24},{18,... | collective-permute-start | bytes 196616 | tf_op jit(solution)/shard_map/ppermute | solution.py:49

commit v3 on v2

--- a/solution.py
+++ b/solution.py
@@ -221,7 +221,7 @@
             sum_ref[j + i] = part
 
 
-def join_kernel(near_ref, far_ref, far_row_ref, _, strips_ref):
+def join_kernel(far_ref, near_ref, far_row_ref, _, strips_ref):
     size = near_ref.shape[0]
     strips_ref[0:size] = near_ref[...]
     strips_ref[size : 2 * size] = far_ref[...]
@@ -352,15 +352,15 @@
     far = exchange(far, "sx", "sy", True)
     (one,) = call(first_kernel, [((half, *taps), f32)], [rows, weight], [xs])
     low, high = call(to_strips, [((strip, lanes), bf16)] * 2, [rows, near, far, one], left={3: ANY})
+    high = exchange(high, "sy", "sx", True)
     low = exchange(low, "sy", "sx", False)
-    high = exchange(high, "sy", "sx", True)
     (two,) = call(
         second_kernel,
         [((cells_x - half, *taps), f32)],
         [rows, near, far, weight],
         [xs],
     )
-    (strips,) = call(join_kernel, [((2 * strip + channels, lanes), bf16)], [low, high, far, two], left={3: ANY})
+    (strips,) = call(join_kernel, [((2 * strip + channels, lanes), bf16)], [high, low, far, two], left={3: ANY})
     other_strips = [lax.ppermute(strips, "ch", along(step)) for step in range(1, count)]
     (ends,) = call(ends_kernel, [((2, outputs, lanes), f32)], [strips, weight, near])
     other_rows, other_near = [], []

time: 22.8 us -> 23.1 us (1.013)
  starting transfers between devices: 6.92 us -> 8.67 us
  waiting for transfers between devices: 1.96 us -> 0.36 us
    ppermute x5, starting transfers between devices: 3.43 us -> 4.99 us  [exchange(): return lax.ppermute(block, ('sx', 'sy'), moves)]
    ppermute x1, waiting for transfers between devices: 0.64 us -> 0.01 us  [per_device(): lax.ppermute(volume, 'ch', along(step))]
    ppermute x1, waiting for transfers between devices: 0.51 us -> 0.01 us  [per_device(): lax.ppermute(strips, 'ch', along(step))]
    ppermute x5, waiting for transfers between devices: 0.81 us -> 0.35 us  [exchange(): return lax.ppermute(block, ('sx', 'sy'), moves)]
  transfers between devices with their start and end apart: 7 -> 7, of which waited for: 3 -> 1; matrix products, arithmetic and copies ran while one was open for 0% -> 0% of each run, Pallas kernels for 44% -> 44%
where the time goes in v3:
time: 23.1 us; the launch traced here: 22.9 us
  Pallas kernels  12.3 us (53%)
  starting transfers between devices  8.67 us (38%)
  local copies, waits for them, and re-layouts  1.34 us (6%)
  waiting for transfers between devices  0.36 us (2%)
    pallas_call x11, Pallas kernels, call(): pl.pallas_call(kernel, out_shape=[jax.ShapeDtypeStruct(s, d) for s, d in...  12.3 us
    ppermute x5, starting transfers between devices, exchange(): return lax.ppermute(block, ('sx', 'sy'), moves)  4.99 us
    ppermute x1, starting transfers between devices, per_device(): lax.ppermute(volume, 'ch', along(step))  2.97 us
    unnamed x8, local copies, waits for them, and re-layouts  1.26 us
    ppermute x1, starting transfers between devices, per_device(): lax.ppermute(strips, 'ch', along(step))  0.71 us
  transfers between devices with their start and end apart: 7, of which 1 were waited for; matrix products, arithmetic and copies ran while one was open for 0% of the time, Pallas kernels for 44%

profile of v3, /device:TPU:0, one launch (start us, length us, event | category | flops | bytes accessed | tf_op | source)
XLA Modules:
  0.0 22.9 jit_solution(120325077870974592)
XLA Ops:
  0.0 0.0 copy-start
  0.0 3.0 %collective-permute-start.2 = (bf16[256,8,128]{2,1,0:T(8,128)(2,1)}, bf16[256,8,128]{2,1,0:T(8,128)(2,1)S(1)}, u32[]{:S(2)}, u32[]{:S(2)}) collective-permute-start(bf16[256,8,128]{2,1,0:T(8,128)(2,1)} %v_ref.1), channel_id=1, source_target_pairs={{0,1},{1,0},{2,3},{3,2},{4,5},{5,4},{6,7},{7,6},{8,9},{9,8},{10,11... | collective-permute-start | bytes 1572872 | tf_op jit(solution)/shard_map/ppermute | solution.py:341
  3.0 0.0 slice-start
  3.0 0.0 copy-done
  3.0 0.0 slice-start.1
  3.0 0.1 shard_map.38
  3.1 0.1 collective-permute-start
  3.2 1.6 %collective-permute-start.1 = (bf16[256,128]{1,0:T(8,128)(2,1)S(1)}, bf16[256,128]{1,0:T(8,128)(2,1)S(1)}, u32[]{:S(2)}, u32[]{:S(2)}) collective-permute-start(bf16[256,128]{1,0:T(8,128)(2,1)S(1)} %get-tuple-element.14), channel_id=1, source_target_pairs={{0,2},{2,0},{4,6},{6,4},{8,16},{10,18},{12,20},{14,22},{16,8},{18,... | collective-permute-start | bytes 196616 | tf_op jit(solution)/shard_map/ppermute | solution.py:49
  4.8 0.3 %slice-done = s8[4194304]{0:T(1024)(128)(4,1)S(1)} async-done(((s8[7077888]{0:T(1024)(128)(4,1)}), s8[4194304]{0:T(1024)(128)(4,1)S(1)}, s32[]{:S(2)}) %slice-start) | async-done | bytes 4194328
  5.2 0.9 %slice-done.1 = s8[2883584]{0:T(1024)(128)(4,1)S(1)} async-done(((s8[7077888]{0:T(1024)(128)(4,1)}), s8[2883584]{0:T(1024)(128)(4,1)S(1)}, s32[]{:S(2)}) %slice-start.1) | async-done | bytes 2883608
  6.1 2.0 %shard_map.39._.refs_1_ = f32[4,768,128]{2,1,0:T(8,128)S(1)} custom-call(bf16[8,256,128]{2,1,0:T(8,128)(2,1)S(1)} %get-tuple-element.12.rows_ref, bf16[3,3,3,256,512]{4,3,2,1,0:T(8,128)(2,1)S(1)} %bitcast.1), custom_call_target="tpu_custom_call" | custom-call | tf_op jit(solution)/shard_map/pallas_call | solution.py:18
  8.1 0.0 collective-permute-done.near_ref
  8.1 0.0 collective-permute-done.1.far_ref.far_row_ref
  8.1 0.5 %shard_map.41 = (bf16[320,128]{1,0:T(8,128)(2,1)S(1)}, bf16[320,128]{1,0:T(8,128)(2,1)S(1)}) custom-call(bf16[8,256,128]{2,1,0:T(8,128)(2,1)S(1)} %get-tuple-element.12.rows_ref, bf16[256,128]{1,0:T(8,128)(2,1)S(1)} %collective-permute-done.near_ref, bf16[256,128]{1,0:T(8,128)(2,1)S(1)} %collective-permute-done.1.far_ref.far_row_ref, ...), custom_call_target="tpu_custom_call" | custom-call | tf_op jit(solution)/shard_map/pallas_call | solution.py:18
  8.6 0.1 collective-permute-start.3
  8.7 3.1 %collective-permute-start.4 = (bf16[320,128]{1,0:T(8,128)(2,1)S(1)}, bf16[320,128]{1,0:T(8,128)(2,1)S(1)}, u32[]{:S(2)}, u32[]{:S(2)}) collective-permute-start(bf16[320,128]{1,0:T(8,128)(2,1)S(1)} %get-tuple-element.16), channel_id=1, source_target_pairs={{0,2},{8,10},{16,18},{24,26},{2,0},{10,8},{18,16},{26,24},{4,6},{1... | collective-permute-start | bytes 245768 | tf_op jit(solution)/shard_map/ppermute | solution.py:49
  11.8 2.1 %shard_map.40._.refs_2_.refs_1_ = f32[4,768,128]{2,1,0:T(8,128)S(1)} custom-call(bf16[8,256,128]{2,1,0:T(8,128)(2,1)S(1)} %get-tuple-element.12.rows_ref, bf16[256,128]{1,0:T(8,128)(2,1)S(1)} %collective-permute-done.near_ref, bf16[256,128]{1,0:T(8,128)(2,1)S(1)} %collective-permute-done.1.far_ref.far_row_ref, bf16[3,3,3,256,512]{4,3,2,1,0:T(8,128)(2,1)S(1)} %bitcast.1), custom_call_target="tpu_custom_call" | custom-call | tf_op jit(solution)/shard_map/pallas_call | solution.py:18
  13.9 0.0 collective-permute-done.3.far_ref
  13.9 0.3 %collective-permute-done.4.near_ref = bf16[320,128]{1,0:T(8,128)(2,1)S(1)} collective-permute-done((bf16[320,128]{1,0:T(8,128)(2,1)S(1)}, bf16[320,128]{1,0:T(8,128)(2,1)S(1)}, u32[]{:S(2)}, u32[]{:S(2)}) %collective-permute-start.4) | collective-permute-done | bytes 81952 | tf_op jit(solution)/shard_map/ppermute | solution.py:49
  14.3 0.0 copy-start.1
  14.3 0.7 %collective-permute-start.6 = (bf16[896,128]{1,0:T(8,128)(2,1)S(1)}, bf16[896,128]{1,0:T(8,128)(2,1)S(1)}, u32[]{:S(2)}, u32[]{:S(2)}) collective-permute-start(bf16[896,128]{1,0:T(8,128)(2,1)S(1)} %shard_map.42.strips_ref), channel_id=1, source_target_pairs={{0,1},{1,0},{2,3},{3,2},{4,5},{5,4},{6,7},{7,6},{8,9},{9,8},{10,11... | collective-permute-start | bytes 688136 | tf_op jit(solution)/shard_map/ppermute | solution.py:364
  15.0 0.9 %shard_map.43.refs_0_.refs_2_ = f32[2,256,128]{2,1,0:T(8,128)S(1)} custom-call(bf16[896,128]{1,0:T(8,128)(2,1)S(1)} %shard_map.42.strips_ref, bf16[3,3,3,256,512]{4,3,2,1,0:T(8,128)(2,1)S(1)} %bitcast.1, bf16[256,128]{1,0:T(8,128)(2,1)S(1)} %collective-permute-done.near_ref), custom_call_target="tpu_custom_call" | custom-call | tf_op jit(solution)/shard_map/pallas_call | solution.py:18
  15.8 0.0 collective-permute-done.2.v_ref
  15.8 0.1 shard_map.44
  16.0 0.1 collective-permute-start.5
  16.0 0.0 copy-done.1
  16.0 0.1 broadcast_in_dim.2.refs_3_.refs_2_
  16.1 3.1 %shard_map.45.refs_3_.refs_0_ = f32[6,256,128]{2,1,0:T(8,128)S(1)} custom-call(bf16[3,3,3,256,512]{4,3,2,1,0:T(8,128)(2,1)S(1)} %bitcast.1, f32[4,768,128]{2,1,0:T(8,128)S(1)} %shard_map.39._.refs_1_, f32[4,768,128]{2,1,0:T(8,128)S(1)} %shard_map.40._.refs_2_.refs_1_, f32[256,128]{1,0:T(8,128)S(1)} %broadcast_in_dim.2.refs_3_.refs_2_, ...), custom_call_target="tpu_custom_call" | custom-call | tf_op jit(solution)/shard_map/pallas_call | solution.py:18
  19.3 0.0 collective-permute-done.5.refs_5_
  19.3 1.3 %shard_map.46.refs_1_ = f32[2,256,128]{2,1,0:T(8,128)S(1)} custom-call(bf16[3,3,3,256,512]{4,3,2,1,0:T(8,128)(2,1)S(1)} %bitcast.1, f32[4,768,128]{2,1,0:T(8,128)S(1)} %shard_map.40._.refs_2_.refs_1_, f32[256,128]{1,0:T(8,128)S(1)} %broadcast_in_dim.2.refs_3_.refs_2_, f32[6,256,128]{2,1,0:T(8,128)S(1)} %shard_map.45.refs_3_.refs_0_, ...), custom_call_target="tpu_custom_call" | custom-call | tf_op jit(solution)/shard_map/pallas_call | solution.py:18
  20.6 0.0 collective-permute-done.6.refs_4_
  20.6 2.2 %shard_map.47 = bf16[256,8,128]{2,1,0:T(8,128)(2,1)} custom-call(f32[6,256,128]{2,1,0:T(8,128)S(1)} %shard_map.45.refs_3_.refs_0_, f32[2,256,128]{2,1,0:T(8,128)S(1)} %shard_map.46.refs_1_, f32[2,256,128]{2,1,0:T(8,128)S(1)} %shard_map.43.refs_0_.refs_2_, bf16[3,3,3,256,512]{4,3,2,1,0:T(8,128)(2,1)S(1)} %bitcast.1, ...), custom_call_target="tpu_custom_call" | custom-call | tf_op jit(solution)/shard_map/pallas_call | solution.py:18
  (3 shorter events, 0.0 us)
Async XLA Ops:
  0.0 3.0 %copy-start = (bf16[256,8,128]{2,1,0:T(8,128)(2,1)S(1)}, bf16[256,8,128]{2,1,0:T(8,128)(2,1)}, u32[]{:S(2)}) copy-start(bf16[256,8,128]{2,1,0:T(8,128)(2,1)} %v_ref.1) | copy-start | bytes 1572868
  0.0 15.8 %collective-permute-start.2 = (bf16[256,8,128]{2,1,0:T(8,128)(2,1)}, bf16[256,8,128]{2,1,0:T(8,128)(2,1)S(1)}, u32[]{:S(2)}, u32[]{:S(2)}) collective-permute-start(bf16[256,8,128]{2,1,0:T(8,128)(2,1)} %v_ref.1), channel_id=1, source_target_pairs={{0,1},{1,0},{2,3},{3,2},{4,5},{5,4},{6,7},{7,6},{8,9},{9,8},{10,11... | collective-permute-start | bytes 1572872 | tf_op jit(solution)/shard_map/ppermute | solution.py:341
  3.0 2.2 %slice-start = ((s8[7077888]{0:T(1024)(128)(4,1)}), s8[4194304]{0:T(1024)(128)(4,1)S(1)}, s32[]{:S(2)}) async-start(s8[7077888]{0:T(1024)(128)(4,1)} %bitcast), calls=%async_computation | async-start | bytes 8388608
  3.0 3.1 %slice-start.1 = ((s8[7077888]{0:T(1024)(128)(4,1)}), s8[2883584]{0:T(1024)(128)(4,1)S(1)}, s32[]{:S(2)}) async-start(s8[7077888]{0:T(1024)(128)(4,1)} %bitcast), calls=%async_computation.1 | async-start | bytes 5767168
  3.1 5.0 %collective-permute-start = (bf16[256,128]{1,0:T(8,128)(2,1)S(1)}, bf16[256,128]{1,0:T(8,128)(2,1)S(1)}, u32[]{:S(2)}, u32[]{:S(2)}) collective-permute-start(bf16[256,128]{1,0:T(8,128)(2,1)S(1)} %get-tuple-element.13), channel_id=1, source_target_pairs={{0,8},{2,10},{4,12},{6,14},{8,0},{10,2},{12,4},{14,6},{16,24},{18,... | collective-permute-start | bytes 196616 | tf_op jit(solution)/shard_map/ppermute | solution.py:49
  3.2 4.9 %collective-permute-start.1 = (bf16[256,128]{1,0:T(8,128)(2,1)S(1)}, bf16[256,128]{1,0:T(8,128)(2,1)S(1)}, u32[]{:S(2)}, u32[]{:S(2)}) collective-permute-start(bf16[256,128]{1,0:T(8,128)(2,1)S(1)} %get-tuple-element.14), channel_id=1, source_target_pairs={{0,2},{2,0},{4,6},{6,4},{8,16},{10,18},{12,20},{14,22},{16,8},{18,... | collective-permute-start | bytes 196616 | tf_op jit(solution)/shard_map/ppermute | solution.py:49
  8.6 5.3 %collective-permute-start.3 = (bf16[320,128]{1,0:T(8,128)(2,1)S(1)}, bf16[320,128]{1,0:T(8,128)(2,1)S(1)}, u32[]{:S(2)}, u32[]{:S(2)}) collective-permute-start(bf16[320,128]{1,0:T(8,128)(2,1)S(1)} %get-tuple-element.15), channel_id=1, source_target_pairs={{0,8},{8,0},{16,24},{24,16},{2,4},{10,12},{18,20},{26,28},{4,2},{1... | collective-permute-start | bytes 245768 | tf_op jit(solution)/shard_map/ppermute | solution.py:49
  8.7 5.6 %collective-permute-start.4 = (bf16[320,128]{1,0:T(8,128)(2,1)S(1)}, bf16[320,128]{1,0:T(8,128)(2,1)S(1)}, u32[]{:S(2)}, u32[]{:S(2)}) collective-permute-start(bf16[320,128]{1,0:T(8,128)(2,1)S(1)} %get-tuple-element.16), channel_id=1, source_target_pairs={{0,2},{8,10},{16,18},{24,26},{2,0},{10,8},{18,16},{26,24},{4,6},{1... | collective-permute-start | bytes 245768 | tf_op jit(solution)/shard_map/ppermute | solution.py:49
  14.3 1.8 %copy-start.1 = (f32[256]{0:T(256)S(1)}, f32[256]{0:T(256)}, u32[]{:S(2)}) copy-start(f32[256]{0:T(256)} %param.5) | copy-start | bytes 3076
  14.3 6.4 %collective-permute-start.6 = (bf16[896,128]{1,0:T(8,128)(2,1)S(1)}, bf16[896,128]{1,0:T(8,128)(2,1)S(1)}, u32[]{:S(2)}, u32[]{:S(2)}) collective-permute-start(bf16[896,128]{1,0:T(8,128)(2,1)S(1)} %shard_map.42.strips_ref), channel_id=1, source_target_pairs={{0,1},{1,0},{2,3},{3,2},{4,5},{5,4},{6,7},{7,6},{8,9},{9,8},{10,11... | collective-permute-start | bytes 688136 | tf_op jit(solution)/shard_map/ppermute | solution.py:364
  16.0 3.3 %collective-permute-start.5 = (bf16[256,128]{1,0:T(8,128)(2,1)S(1)}, bf16[256,128]{1,0:T(8,128)(2,1)S(1)}, u32[]{:S(2)}, u32[]{:S(2)}) collective-permute-start(bf16[256,128]{1,0:T(8,128)(2,1)S(1)} %get-tuple-element.18), channel_id=1, source_target_pairs={{0,8},{2,10},{4,12},{6,14},{8,0},{10,2},{12,4},{14,6},{16,24},{18,... | collective-permute-start | bytes 196616 | tf_op jit(solution)/shard_map/ppermute | solution.py:49
